TPU v7x, 256 devices: a whole 4x4x8 slice. The times are simulated.
256 devices in a mesh: corpus: 16 (over z, core), batch: 4 (over x), tensor: 4 (over y).
Axes of the slice: x: 4, y: 4, z: 8, core: 2. Of those that a mesh axis runs over, the one named last changes fastest.
Arguments:
- states: bfloat16 [4, 32, 256, 768], P('batch', 'corpus'), may hold values from -24 to 24
- token_ids: int32 [4, 32, 256], P('batch', 'corpus'), may hold values from 0 to 50264, as said below
- hop_passages: int32 [4, 32], P('batch'), may hold values from 0 to 131071
- path_question: int32 [4, 32], P('batch'), may hold values from 0 to 15, never falling along the last dimension, each value on 1 to 4 neighbouring positions
- question_vecs: bfloat16 [4, 16, 768], P('batch'), may hold values from -2 to 2
- passage_slab: bfloat16 [131072, 768], P(('corpus', 'tensor')), may hold values from -5 to 5
- w_qkv: bfloat16 [768, 3, 768], P(None, None, 'tensor'), may hold values from -0.21875 to 0.21875
- w_out: bfloat16 [768, 768], P('tensor'), may hold values from -0.21875 to 0.21875
- w_up: bfloat16 [768, 3072], P(None, 'tensor'), may hold values from -0.21875 to 0.21875
- w_down: bfloat16 [3072, 768], P('tensor'), may hold values from -0.109375 to 0.109375
- gain_attn: float32 [768], replicated, may hold values from 0.1 to 1.9
- gain_out: float32 [768], replicated, may hold values from 0.1 to 1.9
Outputs:
- log_probs: float32 [4, 16, 131072], P('batch', None, ('corpus', 'tensor'))
Inputs may be any that keep to these rules, and one draw needn't show every extreme that they name: `token_ids`: position 0 of every text holds 0; id 1 is padding and fills exactly the positions from a text's length on; lengths run from 64 to 256, and texts 0, 2, 4, ... of each mini-batch have no padding.
All inputs are finite; a program needn't handle non-finite values.
Results may differ from a plain program's by a relative error of at most 0.0012.
Values may be sent and summed in bfloat16 or wider, within the bound.
A program may use at most 64 MiB of HBM per device.

v0:
```python
import jax
import jax.numpy as jnp
from jax import lax
from jax.sharding import PartitionSpec as P

HEAD_DIM = 64


epsilon = 1e-05
score_gain = 3.0
column_block = 512


def layer_norm(values, scale_vec):
    centered = values - jnp.mean(values, axis=-1, keepdims=True)
    spread = jnp.mean(centered * centered, axis=-1, keepdims=True)
    return centered * lax.rsqrt(spread + epsilon) * scale_vec


def attend(projected, real_token):
    text_count = real_token.shape[0]
    seq_len = real_token.shape[1]
    heads_here = projected.shape[1] // (3 * HEAD_DIM)
    pieces = projected.reshape(text_count, seq_len, 3, heads_here, HEAD_DIM)
    logits = jnp.einsum(
        "tqhd,tkhd->thqk", pieces[:, :, 0], pieces[:, :, 1], preferred_element_type=jnp.float32
    ) * HEAD_DIM ** (-0.5)
    logits = jnp.where(real_token[:, None, None, :], logits, -jnp.inf)
    largest = jnp.max(logits, axis=-1, keepdims=True)
    weights = jnp.exp(logits - largest)
    weights = (weights / jnp.sum(weights, axis=-1, keepdims=True)).astype(jnp.bfloat16)
    context = jnp.einsum(
        "thqk,tkhd->tqhd", weights, pieces[:, :, 2], preferred_element_type=jnp.float32
    )
    return context.astype(jnp.bfloat16).reshape(text_count * seq_len, heads_here * HEAD_DIM)


def local_context(flat_rows, weight_qkv, real_token):
    width = flat_rows.shape[1]
    projected = jnp.dot(
        flat_rows, weight_qkv.reshape(width, -1), preferred_element_type=jnp.float32
    ).astype(jnp.bfloat16)
    return attend(projected, real_token)


def shards(
    states,
    token_ids,
    hop_passages,
    path_question,
    question_vecs,
    passage_slab,
    w_qkv,
    w_out,
    w_up,
    w_down,
    gain_attn,
    gain_out,
):
    texts_here = states.shape[1]
    seq_len = states.shape[2]
    width = states.shape[3]
    total_rows = texts_here * seq_len
    passages = passage_slab.shape[0]
    questions = question_vecs.shape[1]
    device = lax.axis_index("corpus") * lax.axis_size("tensor") + lax.axis_index("tensor")
    offset = hop_passages[0] - device * passages
    is_owner = (offset >= 0) & (offset < passages)
    picked = jnp.take(passage_slab, jnp.clip(offset, 0, passages - 1), axis=0).astype(jnp.float32)
    member_cols = path_question[0][:, None] == jnp.arange(questions, dtype=jnp.int32)[None, :]
    question_rows = jnp.dot(
        member_cols.astype(jnp.bfloat16), question_vecs[0], preferred_element_type=jnp.float32
    )
    hop_term = jnp.where(is_owner, jnp.sum(picked * question_rows, axis=-1), 0.0)
    hop_score = lax.psum(hop_term, ("corpus", "tensor"))
    real_token = token_ids[0] != 1
    counts = jnp.sum(real_token.astype(jnp.float32), axis=1)
    flat_rows = states.reshape(total_rows, width)
    context = local_context(flat_rows, w_qkv, real_token)
    attended = lax.psum(jnp.dot(context, w_out, preferred_element_type=jnp.float32), "tensor")
    hidden = layer_norm(flat_rows.astype(jnp.float32) + attended, gain_attn).astype(jnp.bfloat16)
    activated = jax.nn.gelu(
        jnp.dot(hidden, w_up, preferred_element_type=jnp.float32), approximate=False
    ).astype(jnp.bfloat16)
    fed_forward = lax.psum(
        jnp.dot(activated, w_down, preferred_element_type=jnp.float32).astype(jnp.bfloat16),
        "tensor",
    ).astype(jnp.float32)
    encoded = layer_norm(hidden.astype(jnp.float32) + fed_forward, gain_out).reshape(
        texts_here, seq_len, width
    )
    pooled_here = jnp.sum(jnp.where(real_token[:, :, None], encoded, 0.0), axis=1) / counts[:, None]
    pooled = lax.all_gather(pooled_here.astype(jnp.bfloat16), "corpus", axis=0, tiled=True)
    pooled_wide = pooled.astype(jnp.float32)
    queries = (
        pooled_wide * lax.rsqrt(jnp.sum(pooled_wide * pooled_wide, axis=-1, keepdims=True) + 1e-06)
    ).astype(jnp.bfloat16)
    direct = jnp.einsum("pd,jd->pj", queries, passage_slab, preferred_element_type=jnp.float32)
    path_scores = hop_score[:, None] + score_gain * direct
    tile_width = min(column_block, passages)
    path_count = path_scores.shape[0]
    member = path_question[0][None, :] == jnp.arange(questions, dtype=jnp.int32)[:, None]
    tile_set = path_scores.reshape(path_count, passages // tile_width, tile_width).transpose(
        1, 0, 2
    )

    def marginal_tile(tile):
        masked = jnp.where(member[:, :, None], tile[None], -jnp.inf)
        largest = jnp.max(masked, axis=1)
        return largest + jnp.log(jnp.sum(jnp.exp(masked - largest[:, None, :]), axis=1))

    marginal = lax.map(marginal_tile, tile_set).transpose(1, 0, 2).reshape(questions, passages)
    local_top = jnp.max(marginal, axis=1)
    local_sum = jnp.sum(jnp.exp(marginal - local_top[:, None]), axis=1)
    overall_top = lax.pmax(local_top, ("corpus", "tensor"))
    totals = lax.psum(local_sum * jnp.exp(local_top - overall_top), ("corpus", "tensor"))
    log_norm = overall_top + jnp.log(totals)
    return (marginal - log_norm[:, None])[None]


def solution(mesh):
    return jax.shard_map(
        shards,
        mesh=mesh,
        in_specs=(
            P("batch", "corpus", None, None),
            P("batch", "corpus", None),
            P("batch", None),
            P("batch", None),
            P("batch", None, None),
            P(("corpus", "tensor"), None),
            P(None, None, "tensor"),
            P("tensor", None),
            P(None, "tensor"),
            P("tensor", None),
            P(),
            P(),
        ),
        out_specs=P("batch", None, ("corpus", "tensor")),
        check_vma=False,
    )
```

profile of v0, /device:TPU:1, one launch (start us, length us, event | category | flops | bytes accessed | tf_op | source)
XLA Modules:
  0.0 496.2 jit_solution(9948090595783866095)
XLA Ops:
  6.5 0.0 copy-start
  6.5 0.0 all-reduce.3.cloned.1.call-start
  6.5 3.0 convolution_convert_fusion.1
  9.6 0.0 copy-start.9
  9.6 2.6 reshape.167
  12.2 2.2 fusion.91
  14.4 0.0 copy-done.9
  14.4 0.1 convert_reduce_fusion
  14.5 3.3 fusion.92
  17.9 1.7 fusion.20
  19.6 0.2 copy.37
  19.8 0.0 copy-done.5
  19.8 1.6 fusion.95
  21.4 0.0 all-reduce.3.cloned.1.call-update
  21.4 0.0 all-reduce.5.cloned.1.call-start
  21.5 59.4 %all-reduce.3.cloned.1.call-done = f32[512,768]{1,0:T(8,128)} async-done(((f32[512,768]{1,0:T(8,128)}), f32[512,768]{1,0:T(8,128)}) %all-reduce.3.cloned.1.call-update) | async-done | bytes 1572880 | tf_op jit(solution)/shard_map/psum | solution.py:80
  80.9 0.0 copy-start.1
  80.9 0.0 copy-start.4
  80.9 2.0 fusion.52
  82.8 0.0 copy-start.7
  82.9 0.1 copy-done.1
  83.0 0.2 copy-done.4
  83.2 0.4 multiply_reduce_fusion.1
  83.6 0.0 copy-done.7
  83.6 1.2 multiply_convert_fusion
  84.9 0.0 copy-start.10
  84.9 7.3 %convolution_convert_fusion = bf16[512,768]{1,0:T(8,128)(2,1)} fusion(bf16[768,768]{1,0:T(8,128)(2,1)} %param.23, bf16[512,768]{1,0:T(8,128)(2,1)} %multiply_convert_fusion, bf16[768,768]{1,0:T(8,128)(2,1)} %param.22), kind=kOutput, calls=%fused_computation.44 | convolution fusion | flops 1233911808 | bytes 3932160 | tf_op jit(solution)/shard_map/dot_general | solution.py:86
  92.2 0.0 all-reduce.5.cloned.1.call-update
  92.2 0.0 copy-done.10
  92.3 0.0 copy-done
  92.3 0.6 gather_fusion
  92.9 0.0 copy-done.6
  92.9 0.0 copy-done.11
  92.9 0.3 fusion.21
  93.3 123.5 %psum.28 = f32[32]{0:T(128)S(1)} all-reduce(f32[32]{0:T(128)S(1)} %bitcast_select_fusion), channel_id=1, replica_groups=mesh['corpus'=16,'batch'=4,'tensor'=4] {'corpus','tensor'}, use_global_device_ids=true, to_apply=%region_1.2 | all-reduce | flops 32 | bytes 256 | tf_op jit(solution)/shard_map/psum | solution.py:75
  216.8 0.0 all-reduce.5.cloned.1.call-done
  216.8 0.0 copy-start.2
  216.8 0.0 copy-start.3
  216.8 1.8 fusion.19
  218.6 0.0 copy-done.2
  218.6 0.0 copy-done.3
  218.7 0.4 multiply_reduce_fusion
  219.1 0.0 copy-done.8
  219.1 0.5 select_reduce_fusion.1
  219.5 0.1 fusion.56
  219.6 19.1 %all-gather = bf16[16,2,768]{2,1,0:T(2,128)(2,1)S(1)} all-gather(bf16[1,2,768]{2,1,0:T(2,128)(2,1)S(1)} %fusion.56), channel_id=1, replica_groups=mesh['corpus'=16,'batch'=4,'tensor'=4] {'corpus'}, dimensions={0}, use_global_device_ids=true | all-gather | bytes 52224 | tf_op jit(solution)/shard_map/all_gather | solution.py:93
  238.7 0.1 multiply_reduce_fusion.2
  238.9 1.0 fusion.5
  239.9 2.6 while.11
  240.0 0.2 select_reduce_fusion.3
  240.2 0.3 fusion.105
  240.6 0.2 select_reduce_fusion.3
  240.9 0.3 fusion.105
  241.3 0.2 select_reduce_fusion.3
  241.5 0.3 fusion.105
  241.9 0.2 select_reduce_fusion.3
  242.2 0.3 fusion.105
  242.5 0.1 reduce_max.28
  242.7 0.2 exponential_reduce_fusion
  242.9 119.9 %pmax.7 = f32[16]{0:T(128)S(1)} all-reduce(f32[16]{0:T(128)S(1)} %reduce_max.28), channel_id=1, replica_groups=mesh['corpus'=16,'batch'=4,'tensor'=4] {'corpus','tensor'}, use_global_device_ids=true, to_apply=%region_18.19 | all-reduce | flops 16 | bytes 128 | tf_op jit(solution)/shard_map/pmax | solution.py:115
  362.8 125.7 %psum.31 = f32[16]{0:T(128)S(1)} all-reduce(f32[16]{0:T(128)S(1)} %exponential_multiply_fusion), channel_id=1, replica_groups=mesh['corpus'=16,'batch'=4,'tensor'=4] {'corpus','tensor'}, use_global_device_ids=true, to_apply=%region_20.21 | all-reduce | flops 16 | bytes 128 | tf_op jit(solution)/shard_map/psum | solution.py:116
  488.5 0.1 copy.39
  488.6 0.1 reshape.171
  488.7 0.7 broadcast_subtract_fusion
  (31 shorter events, 0.3 us)
Async XLA Ops:
  6.5 85.7 %copy-start = (bf16[2048,768]{1,0:T(8,128)(2,1)S(1)}, bf16[2048,768]{1,0:T(8,128)(2,1)}, u32[]{:S(2)}) copy-start(bf16[2048,768]{1,0:T(8,128)(2,1)} %param.19) | copy-start | bytes 9437188
  6.5 74.3 %all-reduce.3.cloned.1.call-start = ((), (), s32[]{:S(2)}) async-start(), calls=%async_computation | async-start | bytes 3145728 | tf_op jit(solution)/shard_map/psum | solution.py:80
  9.6 4.9 copy-start.9
  17.9 1.9 copy-start.5
  21.4 195.4 %all-reduce.5.cloned.1.call-start = ((), (), s32[]{:S(2)}) async-start(), calls=%async_computation.1 | async-start | bytes 1572864 | tf_op jit(solution)/shard_map/psum | solution.py:85
  80.9 2.1 copy-start.1
  80.9 2.3 copy-start.4
  82.8 0.8 copy-start.7
  84.9 7.4 %copy-start.10 = (s32[1,32]{1,0:T(1,128)S(1)}, s32[1,32]{1,0:T(1,128)}, u32[]{:S(2)}) copy-start(s32[1,32]{1,0:T(1,128)} %param.16) | copy-start | bytes 388
  84.9 8.1 %copy-start.6 = (s32[1,32]{1,0:T(1,128)S(1)}, s32[1,32]{1,0:T(1,128)}, u32[]{:S(2)}) copy-start(s32[1,32]{1,0:T(1,128)} %param.17) | copy-start | bytes 388
  84.9 8.1 %copy-start.11 = (bf16[1,16,768]{2,1,0:T(8,128)(2,1)S(1)}, bf16[1,16,768]{2,1,0:T(8,128)(2,1)}, u32[]{:S(2)}) copy-start(bf16[1,16,768]{2,1,0:T(8,128)(2,1)} %param.18) | copy-start | bytes 73732
  216.8 2.3 copy-start.8
  216.8 1.8 copy-start.2
  216.8 1.8 copy-start.3
Sparse Core Ops, SparseCore 0:
  21.5 59.2 all-reduce.2
  92.3 48.0 all-reduce.4
where the time goes:
time: 500 us; the launch traced here: 496 us
  blocking collectives  388 us (78%)
  waiting for transfers between devices  59.4 us (12%)
  matrix products  18.3 us (4%)
  between operations  13.6 us (3%)
  other arithmetic  10.1 us (2%)
  local copies, waits for them, and re-layouts  6.37 us (1%)
    psum x1, blocking collectives, shards(): lax.psum(local_sum * jnp.exp(local_top - overall_top), ('corpus', 'tensor'))  126 us
    psum x1, blocking collectives, shards(): hop_score = lax.psum(hop_term, ('corpus', 'tensor'))  124 us
    pmax x1, blocking collectives, shards(): overall_top = lax.pmax(local_top, ('corpus', 'tensor'))  120 us
    psum x1, waiting for transfers between devices, shards(): lax.psum(jnp.dot(context, w_out, preferred_element_type=jnp.float32), 'te...  59.4 us
    all_gather x1, blocking collectives, shards(): lax.all_gather(pooled_here.astype(jnp.bfloat16), 'corpus', axis=0, tiled=...  19.1 us
  transfers between devices with their start and end apart: 2, of which 1 were waited for; matrix products, arithmetic and copies ran while one was open for 0% of the time, Pallas kernels for 0%

commit v1 on v0

v1 whole, which is shorter than its diff:
```python
import functools

import jax
import jax.numpy as jnp
from jax import lax
from jax.experimental import pallas as pl
from jax.experimental.pallas import tpu as pltpu
from jax.sharding import PartitionSpec as P

HEAD_DIM = 64
HOPS = 4
MESH = pl.DeviceIdType.MESH
F32 = jnp.float32
BF16 = jnp.bfloat16

epsilon = 1e-05
score_gain = 3.0


def dot(a, b, ca, cb):
    return lax.dot_general(a, b, (((ca,), (cb,)), ((), ())), preferred_element_type=F32)


def layer_norm(values, scale_row):
    centered = values - jnp.mean(values, axis=-1, keepdims=True)
    spread = jnp.mean(centered * centered, axis=-1, keepdims=True)
    return centered * lax.rsqrt(spread + epsilon) * scale_row


def gelu(v):
    return 0.5 * v * (1.0 + lax.erf(v * (0.5 ** 0.5)))


def iota(shape, dim):
    return lax.broadcasted_iota(jnp.int32, shape, dim)


def col_to_row(col, width):
    n = col.shape[0]
    same = iota((n, width), 0) == iota((n, width), 1)
    return jnp.sum(jnp.where(same, col, jnp.zeros_like(col)), axis=0, keepdims=True)


def row_to_col(row, n):
    width = row.shape[1]
    same = iota((n, width), 0) == iota((n, width), 1)
    return jnp.sum(jnp.where(same, row, jnp.zeros_like(row)), axis=1, keepdims=True)


def kernel(
    sizes,
    tok_ref, hop_ref, pq_ref, qv_ref, gain_a_ref, gain_o_ref,
    x_hbm, wqkv_hbm, wout_hbm, wup_hbm, wdown_hbm, slab_hbm,
    out_ref,
    x, wqkv, wout, wup, wdown, slab,
    qkv, ctx, hid, act, ffp, ffr, encs, pool_y, pool_c, hop_y, hop_c, lse_y, lse_c,
    load_sem, w1s, w1r, w2s, w2r, w3s, w3r, cs, cr, fs, fr,
    hys, hyr, hcs, hcr, pys, pyr, pcs, pcr, lys, lyr, lcs, lcr,
):
    n_corpus, n_batch, n_tensor, texts, seq, width = sizes
    c = lax.axis_index("corpus")
    b = lax.axis_index("batch")
    t = lax.axis_index("tensor")
    core = lax.rem(c, 2)
    sibling = c + 1 - 2 * core
    heads_here = wqkv.shape[0] // (3 * HEAD_DIM)
    inner = heads_here * HEAD_DIM
    rows = seq // n_tensor
    ff_here = wup.shape[1]
    passages = slab.shape[0]
    questions = qv_ref.shape[0]
    paths = n_corpus * texts
    own_pass = (c * n_tensor + t) * passages

    def y_peer(d):
        return (c, b, lax.rem(t + d, n_tensor))

    def x_peer(f):
        return (c, lax.rem(b + f, n_batch), t)

    def c_peer(e):
        return (lax.rem(c + e, n_corpus), b, t)

    def remote(src, dst, s, r, dev):
        return pltpu.make_async_remote_copy(
            src_ref=src, dst_ref=dst, send_sem=s, recv_sem=r, device_id=dev, device_id_type=MESH
        )

    loads = []
    for i, (src, dst) in enumerate((
        (x_hbm, x), (wqkv_hbm, wqkv), (wout_hbm, wout.at[0]), (wup_hbm, wup), (wdown_hbm, wdown), (slab_hbm, slab),
    )):
        copy = pltpu.make_async_copy(src, dst, load_sem.at[i])
        copy.start()
        loads.append(copy)
    load_x, load_qkv, load_out, load_up, load_down, load_slab = loads

    barrier = pltpu.get_barrier_semaphore()
    peers = (
        [y_peer(d) for d in range(1, n_tensor)]
        + [x_peer(f) for f in range(1, n_batch)]
        + [c_peer(e) for e in range(1, n_corpus)]
    )
    for dev in peers:
        pl.semaphore_signal(barrier, inc=1, device_id=dev, device_id_type=MESH)
    pl.semaphore_wait(barrier, len(peers))

    piece = inner // n_batch
    half = width // 2
    piece_rows = pl.ds(pl.multiple_of(b * piece, 16), piece)
    half_cols = pl.ds(pl.multiple_of(core * half, 128), half)
    load_out.wait()
    leg1 = [
        remote(
            wout.at[0, piece_rows, half_cols], wout.at[d, piece_rows, half_cols],
            w1s.at[d - 1], w1r.at[d - 1], y_peer(d),
        )
        for d in range(1, n_tensor)
    ]
    for copy in leg1:
        copy.start()

    load_x.wait()
    load_qkv.wait()
    qkv[...] = dot(wqkv[...], x[...], 1, 1).astype(BF16)

    for copy in leg1:
        copy.wait_recv()
    leg2 = [
        remote(
            wout.at[1:n_tensor, piece_rows, half_cols], wout.at[1:n_tensor, piece_rows, half_cols],
            w2s.at[f - 1], w2r.at[f - 1], x_peer(f),
        )
        for f in range(1, n_batch)
    ]
    for copy in leg2:
        copy.start()

    real = tok_ref[...] != 1
    counts = jnp.sum(real.astype(F32), axis=1, keepdims=True)

    ctx_sends = []
    for i in range(texts):
        cols = slice(i * seq, (i + 1) * seq)
        keep = iota((seq, 1), 0).astype(F32) < counts[i:i + 1, :]
        for h in range(heads_here):
            lo = h * HEAD_DIM
            q = qkv[lo:lo + HEAD_DIM, cols] * jnp.asarray(HEAD_DIM ** -0.5, BF16)
            k = qkv[inner + lo:inner + lo + HEAD_DIM, cols]
            v = qkv[2 * inner + lo:2 * inner + lo + HEAD_DIM, cols]
            logits = dot(k, q, 0, 0)
            logits = jnp.where(keep, logits, -jnp.inf)
            weights = jnp.exp(logits - jnp.max(logits, axis=0, keepdims=True))
            weights = (weights * (1.0 / jnp.sum(weights, axis=0, keepdims=True))).astype(BF16)
            ctx[0, i, lo:lo + HEAD_DIM, :] = dot(v, weights, 1, 0).astype(BF16)
        for d in range(1, n_tensor):
            copy = remote(ctx.at[0, i], ctx.at[d, i], cs.at[i, d - 1], cr.at[i, d - 1], y_peer(d))
            copy.start()
            ctx_sends.append(copy)

    for copy in leg2:
        copy.wait_recv()
    leg3 = remote(
        wout.at[1:n_tensor, :, half_cols], wout.at[1:n_tensor, :, half_cols],
        w3s, w3r, (sibling, b, t),
    )
    leg3.start()

    load_slab.wait()
    pq = pq_ref[...]
    member = iota((questions, paths), 0) == pq
    before = jnp.sum((pq < iota((questions, paths), 0)).astype(F32), axis=1, keepdims=True)
    amount = jnp.sum(member.astype(F32), axis=1, keepdims=True)
    hop_col = row_to_col(hop_ref[...].astype(F32), paths)
    here = iota((paths, passages), 1).astype(F32) == hop_col - own_pass.astype(F32)
    picked = dot(here.astype(F32).astype(BF16), slab[...], 1, 0)
    question_rows = dot(member.astype(F32).astype(BF16), qv_ref[...], 0, 0)
    hop_y[0] = col_to_row(jnp.sum(picked * question_rows, axis=1, keepdims=True), 128)
    hop_sends = [
        remote(hop_y.at[0], hop_y.at[d], hys.at[d - 1], hyr.at[d - 1], y_peer(d)) for d in range(1, n_tensor)
    ]
    for copy in hop_sends:
        copy.start()

    leg3.wait_recv()
    load_up.wait()
    load_down.wait()
    ff_sends = []
    for i in range(texts):
        text_rows = slice(i * seq, (i + 1) * seq)
        attended = x[text_rows, :].astype(F32)
        for d in range(n_tensor):
            if d:
                ctx_sends[i * (n_tensor - 1) + d - 1].wait_recv()
            attended = attended + dot(ctx[d, i], wout[d], 0, 0)
        hid[text_rows, :] = layer_norm(attended, gain_a_ref[...]).astype(BF16)
        for n in range(0, ff_here, 256):
            up = dot(hid[text_rows, :], wup[:, n:n + 256], 1, 0)
            act[:, n:n + 256] = gelu(up).astype(BF16)
        ffp[i] = dot(act[...], wdown[...], 1, 0).astype(BF16)
        for d in range(1, n_tensor):
            owner = lax.rem(t + d, n_tensor)
            copy = remote(
                ffp.at[i, pl.ds(pl.multiple_of(owner * rows, 16), rows)], ffr.at[i, d - 1],
                fs.at[i, d - 1], fr.at[i, d - 1], y_peer(d),
            )
            copy.start()
            ff_sends.append(copy)
        if i == 0:
            for copy in hop_sends:
                copy.wait_recv()
            hop_c[0] = jnp.sum(hop_y[...], axis=0)
            hopc_sends = [
                remote(hop_c.at[0], hop_c.at[e], hcs.at[e - 1], hcr, c_peer(e)) for e in range(1, n_corpus)
            ]
            for copy in hopc_sends:
                copy.start()

    for i in range(texts):
        own = pl.ds(pl.multiple_of(t * rows, 16), rows)
        own_hid = pl.ds(pl.multiple_of(i * seq + t * rows, 16), rows)
        total = hid[own_hid, :].astype(F32) + ffp[i, own, :].astype(F32)
        for d in range(1, n_tensor):
            ff_sends[i * (n_tensor - 1) + d - 1].wait_recv()
            total = total + ffr[i, d - 1].astype(F32)
        encoded = layer_norm(total, gain_o_ref[...])
        keep = (t * rows + iota((rows, 1), 0)).astype(F32) < counts[i:i + 1, :]
        pool_y[0, i:i + 1, :] = jnp.sum(jnp.where(keep, encoded, 0.0), axis=0, keepdims=True) / counts[i:i + 1, :]
    pool_sends = [
        remote(pool_y.at[0], pool_y.at[d], pys.at[d - 1], pyr.at[d - 1], y_peer(d)) for d in range(1, n_tensor)
    ]
    for copy in pool_sends:
        copy.start()
    for copy in pool_sends:
        copy.wait_recv()
    pool_c[0] = jnp.sum(pool_y[...], axis=0).astype(BF16).astype(F32)
    poolc_sends = [
        remote(pool_c.at[0], pool_c.at[e], pcs.at[e - 1], pcr, c_peer(e)) for e in range(1, n_corpus)
    ]
    for copy in poolc_sends:
        copy.start()

    rest = n_corpus - 1
    remote(hop_c.at[pl.ds(1, rest)], hop_c.at[pl.ds(1, rest)], hcs.at[0], hcr, c_peer(1)).wait_recv()
    hop_row = jnp.sum(hop_c[...], axis=0)[:, :paths]
    path_at = iota((questions, paths), 1).astype(F32)
    slot = iota((questions, paths), 1)
    slot_path = lax.rem(2 * paths + texts * c - slot + 2 * lax.rem(slot, texts), paths).astype(F32)
    hops, valid, picks = [], [], []
    for k in range(HOPS):
        ok = amount > k
        hops.append(jnp.sum(jnp.where(path_at == before + k, hop_row, 0.0), axis=1, keepdims=True))
        valid.append(ok)
        picks.append(jnp.where((slot_path == before + k) & ok, 1.0, 0.0))
    pick = jnp.concatenate(picks, axis=0).astype(BF16)

    remote(pool_c.at[pl.ds(1, rest)], pool_c.at[pl.ds(1, rest)], pcs.at[0], pcr, c_peer(1)).wait_recv()
    pooled = pool_c[...].reshape(paths, width)
    queries = (pooled * lax.rsqrt(jnp.sum(pooled * pooled, axis=-1, keepdims=True) + 1e-06)).astype(BF16)
    chosen = dot(pick, queries, 1, 0).astype(BF16)
    direct = dot(chosen, slab[...], 1, 1)
    scores = [
        jnp.where(valid[k], hops[k] + score_gain * direct[k * questions:(k + 1) * questions], -jnp.inf)
        for k in range(HOPS)
    ]
    top = functools.reduce(jnp.maximum, scores)
    marginal = top + jnp.log(sum(jnp.exp(s - top) for s in scores))
    local_top = jnp.max(marginal, axis=1, keepdims=True)
    local_lse = local_top + jnp.log(jnp.sum(jnp.exp(marginal - local_top), axis=1, keepdims=True))

    lse_y[0] = col_to_row(local_lse, 128)
    lse_sends = [
        remote(lse_y.at[0], lse_y.at[d], lys.at[d - 1], lyr.at[d - 1], y_peer(d)) for d in range(1, n_tensor)
    ]
    for copy in lse_sends:
        copy.start()
    for copy in lse_sends:
        copy.wait_recv()
    parts = lse_y[...]
    most = jnp.max(parts, axis=0)
    lse_c[0] = most + jnp.log(jnp.sum(jnp.exp(parts - most[None]), axis=0))
    lsec_sends = [
        remote(lse_c.at[0], lse_c.at[e], lcs.at[e - 1], lcr, c_peer(e)) for e in range(1, n_corpus)
    ]
    for copy in lsec_sends:
        copy.start()
    remote(lse_c.at[pl.ds(1, rest)], lse_c.at[pl.ds(1, rest)], lcs.at[0], lcr, c_peer(1)).wait_recv()
    parts = lse_c[...]
    most = jnp.max(parts, axis=0)
    norm = most + jnp.log(jnp.sum(jnp.exp(parts - most[None]), axis=0))
    out_ref[...] = marginal - row_to_col(norm, questions)

    leg3.wait_send()
    for group in (leg1, leg2, ctx_sends, hop_sends, hopc_sends, ff_sends, pool_sends, poolc_sends, lse_sends, lsec_sends):
        for copy in group:
            copy.wait_send()


def shards(mesh_sizes, states, token_ids, hop_passages, path_question, question_vecs, passage_slab,
           w_qkv, w_out, w_up, w_down, gain_attn, gain_out):
    n_corpus, n_batch, n_tensor = mesh_sizes
    texts, seq, width = states.shape[1:]
    total = texts * seq
    passages = passage_slab.shape[0]
    questions = question_vecs.shape[1]
    inner = w_qkv.shape[2]
    ff_here = w_up.shape[1]
    sizes = (n_corpus, n_batch, n_tensor, texts, seq, width)
    ny, nx, nc = n_tensor - 1, n_batch - 1, n_corpus - 1
    dma = pltpu.SemaphoreType.DMA
    vmem = pl.BlockSpec(memory_space=pltpu.VMEM)
    hbm = pl.BlockSpec(memory_space=pl.ANY)
    result = pl.pallas_call(
        functools.partial(kernel, sizes),
        out_shape=jax.ShapeDtypeStruct((questions, passages), F32),
        in_specs=[vmem] * 6 + [hbm] * 6,
        out_specs=vmem,
        scratch_shapes=[
            pltpu.VMEM((total, width), BF16),
            pltpu.VMEM((3 * inner, width), BF16),
            pltpu.VMEM((n_tensor, inner, width), BF16),
            pltpu.VMEM((width, ff_here), BF16),
            pltpu.VMEM((ff_here, width), BF16),
            pltpu.VMEM((passages, width), BF16),
            pltpu.VMEM((3 * inner, total), BF16),
            pltpu.VMEM((n_tensor, texts, inner, seq), BF16),
            pltpu.VMEM((total, width), BF16),
            pltpu.VMEM((seq, ff_here), BF16),
            pltpu.VMEM((texts, seq, width), BF16),
            pltpu.VMEM((texts, ny, seq // n_tensor, width), BF16),
            pltpu.VMEM((8, 128), F32),
            pltpu.VMEM((n_tensor, texts, width), F32),
            pltpu.VMEM((n_corpus, texts, width), F32),
            pltpu.VMEM((n_tensor, 1, 128), F32),
            pltpu.VMEM((n_corpus, 1, 128), F32),
            pltpu.VMEM((n_tensor, 1, 128), F32),
            pltpu.VMEM((n_corpus, 1, 128), F32),
            dma((6,)),
            dma((ny,)), dma((ny,)), dma((nx,)), dma((nx,)), dma, dma,
            dma((texts, ny)), dma((texts, ny)), dma((texts, ny)), dma((texts, ny)),
            dma((ny,)), dma((ny,)), dma((nc,)), dma,
            dma((ny,)), dma((ny,)), dma((nc,)), dma,
            dma((ny,)), dma((ny,)), dma((nc,)), dma,
        ],
        compiler_params=pltpu.CompilerParams(
            collective_id=0, has_side_effects=True, vmem_limit_bytes=48 * 1024 * 1024
        ),
        name="hop_two",
    )(
        token_ids[0], hop_passages, path_question, question_vecs[0],
        gain_attn[None], gain_out[None],
        states.reshape(total, width), jnp.transpose(w_qkv, (1, 2, 0)).reshape(3 * inner, width),
        w_out, w_up, w_down, passage_slab,
    )
    return result[None]


def solution(mesh):
    mesh_sizes = (mesh.shape["corpus"], mesh.shape["batch"], mesh.shape["tensor"])
    return jax.shard_map(
        functools.partial(shards, mesh_sizes),
        mesh=mesh,
        in_specs=(
            P("batch", "corpus", None, None),
            P("batch", "corpus", None),
            P("batch", None),
            P("batch", None),
            P("batch", None, None),
            P(("corpus", "tensor"), None),
            P(None, None, "tensor"),
            P("tensor", None),
            P(None, "tensor"),
            P("tensor", None),
            P(),
            P(),
        ),
        out_specs=P("batch", None, ("corpus", "tensor")),
        check_vma=False,
    )
```

time: 500 us -> 67.3 us (0.13)
  blocking collectives: 388 us -> 0 us
  waiting for transfers between devices: 59.4 us -> 0 us
  Pallas kernels: 0 us -> 56.2 us
  matrix products: 18.3 us -> 0 us
  between operations: 13.6 us -> 0.02 us
  other arithmetic: 10.1 us -> 0 us
    psum x2 -> x0, blocking collectives: 249 us -> none  [the longest x1 126 us: shards(): lax.psum(local_sum * jnp.exp(local_top - overall_top), ('corpus', 'tensor'))]
    pmax x1 -> x0, blocking collectives: 120 us -> none  [shards(): overall_top = lax.pmax(local_top, ('corpus', 'tensor'))]
    psum x2 -> x0, waiting for transfers between devices: 59.4 us -> none  [the longest x1 59.4 us: shards(): lax.psum(jnp.dot(context, w_out, preferred_element_type=jnp.float32), 'te...]
    pallas_call x0 -> x1, Pallas kernels: none -> 56.2 us  [shards(): pl.pallas_call(functools.partial(kernel, sizes), out_shape=jax.ShapeDtype...]
    all_gather x1 -> x0, blocking collectives: 19.1 us -> none  [shards(): lax.all_gather(pooled_here.astype(jnp.bfloat16), 'corpus', axis=0, tiled=...]
    dot_general x6 -> x0, matrix products: 14.9 us -> none  [the longest x1 7.33 us: shards(): jnp.dot(activated, w_down, preferred_element_type=jnp.float32)]
    unnamed x25 -> x19, local copies, waits for them, and re-layouts: 0.43 us -> 9.19 us
    reduce_sum x12 -> x0, other arithmetic: 6.83 us -> none  [the longest x2 3.75 us: layer_norm(): centered = values - jnp.mean(values, axis=-1, keepdims=True)]
  transfers between devices with their start and end apart: 2 -> 0, of which waited for: 1 -> 0; matrix products, arithmetic and copies ran while one was open for 0% -> 0% of each run, Pallas kernels for 0% -> 0%
where the time goes in v1:
time: 67.3 us; the launch traced here: 66.8 us
  Pallas kernels  56.2 us (84%)
  local copies, waits for them, and re-layouts  10.6 us (16%)
    pallas_call x1, Pallas kernels, shards(): pl.pallas_call(functools.partial(kernel, sizes), out_shape=jax.ShapeDtype...  56.2 us
    unnamed x19, local copies, waits for them, and re-layouts  9.19 us

profile of v1, /device:TPU:1, one launch (start us, length us, event | category | flops | bytes accessed | tf_op | source)
XLA Modules:
  0.0 66.8 jit_solution(8597808981852078197)
XLA Ops:
  0.0 0.7 %broadcast_in_dim.9.gain_a_ref = f32[1,768]{1,0:T(1,128)S(1)} reshape(f32[768]{0:T(1024)} %param.22) | data formatting | bytes 6144 | tf_op jit(solution)/shard_map/broadcast_in_dim | solution.py:351
  0.7 0.7 %broadcast_in_dim.10.gain_o_ref = f32[1,768]{1,0:T(1,128)S(1)} reshape(f32[768]{0:T(1024)} %param.23) | data formatting | bytes 6144 | tf_op jit(solution)/shard_map/broadcast_in_dim | solution.py:351
  1.4 0.0 copy-start
  1.4 1.3 %copy-done = bf16[768,768]{1,0:T(8,128)(2,1)S(1)} copy-done((bf16[768,768]{1,0:T(8,128)(2,1)S(1)}, bf16[768,768]{1,0:T(8,128)(2,1)}, u32[]{:S(2)}) %copy-start) | copy-done | bytes 1179672
  2.7 0.0 copy-start.1
  2.7 1.3 %copy-done.1 = bf16[768,768]{1,0:T(8,128)(2,1)S(1)} copy-done((bf16[768,768]{1,0:T(8,128)(2,1)S(1)}, bf16[768,768]{1,0:T(8,128)(2,1)}, u32[]{:S(2)}) %copy-start.1) | copy-done | bytes 1179672
  3.9 0.0 copy-start.2
  3.9 1.2 %copy-done.2 = bf16[768,3,192]{0,2,1:T(8,128)(2,1)S(1)} copy-done((bf16[768,3,192]{0,2,1:T(8,128)(2,1)S(1)}, bf16[768,3,192]{0,2,1:T(8,128)(2,1)}, u32[]{:S(2)}) %copy-start.2) | copy-done | bytes 884760
  5.1 0.0 copy-start.3
  5.1 1.1 %copy-done.3 = bf16[1,2,256,768]{3,2,1,0:T(8,128)(2,1)S(1)} copy-done((bf16[1,2,256,768]{3,2,1,0:T(8,128)(2,1)S(1)}, bf16[1,2,256,768]{3,2,1,0:T(8,128)(2,1)}, u32[]{:S(2)}) %copy-start.3) | copy-done | bytes 786456
  6.2 0.0 copy-start.4
  6.2 1.0 %copy-done.4 = bf16[192,768]{1,0:T(8,128)(2,1)S(1)} copy-done((bf16[192,768]{1,0:T(8,128)(2,1)S(1)}, bf16[192,768]{1,0:T(8,128)(2,1)}, u32[]{:S(2)}) %copy-start.4) | copy-done | bytes 294936
  7.2 0.0 copy-start.5
  7.2 0.7 %copy-done.5 = bf16[1,16,768]{2,1,0:T(8,128)(2,1)S(1)} copy-done((bf16[1,16,768]{2,1,0:T(8,128)(2,1)S(1)}, bf16[1,16,768]{2,1,0:T(8,128)(2,1)}, u32[]{:S(2)}) %copy-start.5) | copy-done | bytes 24600
  7.9 0.0 copy-start.6
  7.9 0.7 %copy-done.6 = s32[1,2,256]{2,1,0:T(2,128)S(1)} copy-done((s32[1,2,256]{2,1,0:T(2,128)S(1)}, s32[1,2,256]{2,1,0:T(2,128)}, u32[]{:S(2)}) %copy-start.6) | copy-done | bytes 2072
  8.6 0.0 copy-start.7
  8.6 0.7 copy-done.7
  9.3 0.0 copy-start.8
  9.3 0.7 copy-done.8
  9.9 56.2 %hop_two.1 = f32[16,2048]{1,0:T(8,128)S(1)} custom-call(s32[2,256]{1,0:T(2,128)S(1)} %bitcast.11, s32[1,32]{1,0:T(1,128)S(1)} %copy-done.7, s32[1,32]{1,0:T(1,128)S(1)} %copy-done.8, bf16[16,768]{1,0:T(8,128)(2,1)S(1)} %bitcast.10, f32[1,768]{1,0:T(1,128)S(1)} %broadcast_in_dim.9.gain_a_ref, f32[1,768]{1,0:T(1,128)S(1)} %broadcast_in_dim.10.gain_o_ref, ...), custom_call_target="tpu_custom_call" | custom-call | tf_op jit(solution)/shard_map/hop_two/pallas_call | solution.py:313
  66.2 0.7 copy.14
Async XLA Ops:
  1.4 1.3 %copy-start = (bf16[768,768]{1,0:T(8,128)(2,1)S(1)}, bf16[768,768]{1,0:T(8,128)(2,1)}, u32[]{:S(2)}) copy-start(bf16[768,768]{1,0:T(8,128)(2,1)} %wup_hbm.1) | copy-start | bytes 3538948
  2.7 1.3 %copy-start.1 = (bf16[768,768]{1,0:T(8,128)(2,1)S(1)}, bf16[768,768]{1,0:T(8,128)(2,1)}, u32[]{:S(2)}) copy-start(bf16[768,768]{1,0:T(8,128)(2,1)} %wdown_hbm.1) | copy-start | bytes 3538948
  3.9 1.2 %copy-start.2 = (bf16[768,3,192]{0,2,1:T(8,128)(2,1)S(1)}, bf16[768,3,192]{0,2,1:T(8,128)(2,1)}, u32[]{:S(2)}) copy-start(bf16[768,3,192]{0,2,1:T(8,128)(2,1)} %param.18) | copy-start | bytes 2654212
  5.1 1.1 %copy-start.3 = (bf16[1,2,256,768]{3,2,1,0:T(8,128)(2,1)S(1)}, bf16[1,2,256,768]{3,2,1,0:T(8,128)(2,1)}, u32[]{:S(2)}) copy-start(bf16[1,2,256,768]{3,2,1,0:T(8,128)(2,1)} %param.12) | copy-start | bytes 2359300
  6.2 1.0 %copy-start.4 = (bf16[192,768]{1,0:T(8,128)(2,1)S(1)}, bf16[192,768]{1,0:T(8,128)(2,1)}, u32[]{:S(2)}) copy-start(bf16[192,768]{1,0:T(8,128)(2,1)} %wout_hbm.1) | copy-start | bytes 884740
  7.2 0.7 %copy-start.5 = (bf16[1,16,768]{2,1,0:T(8,128)(2,1)S(1)}, bf16[1,16,768]{2,1,0:T(8,128)(2,1)}, u32[]{:S(2)}) copy-start(bf16[1,16,768]{2,1,0:T(8,128)(2,1)} %param.16) | copy-start | bytes 73732
  7.9 0.7 %copy-start.6 = (s32[1,2,256]{2,1,0:T(2,128)S(1)}, s32[1,2,256]{2,1,0:T(2,128)}, u32[]{:S(2)}) copy-start(s32[1,2,256]{2,1,0:T(2,128)} %param.13) | copy-start | bytes 6148
  8.6 0.7 copy-start.7
  9.3 0.7 copy-start.8

commit v2 on v1

v2 whole, which is shorter than its diff:
```python
import functools

import jax
import jax.numpy as jnp
from jax import lax
from jax.experimental import pallas as pl
from jax.experimental.pallas import tpu as pltpu
from jax.sharding import PartitionSpec as P

HEAD_DIM = 64
HOPS = 4
PIECE = 128
MESH = pl.DeviceIdType.MESH
F32 = jnp.float32
BF16 = jnp.bfloat16

epsilon = 1e-05
score_gain = 3.0


def dot(a, b, ca, cb):
    return lax.dot_general(a, b, (((ca,), (cb,)), ((), ())), preferred_element_type=F32)


def layer_norm(values, scale_row):
    centered = values - jnp.mean(values, axis=-1, keepdims=True)
    spread = jnp.mean(centered * centered, axis=-1, keepdims=True)
    return centered * lax.rsqrt(spread + epsilon) * scale_row


def gelu(v):
    return 0.5 * v * (1.0 + lax.erf(v * (0.5 ** 0.5)))


def iota(shape, dim):
    return lax.broadcasted_iota(jnp.int32, shape, dim)


def col_to_row(col, width):
    n = col.shape[0]
    same = iota((n, width), 0) == iota((n, width), 1)
    return jnp.sum(jnp.where(same, col, jnp.zeros_like(col)), axis=0, keepdims=True)


def row_to_col(row, n):
    width = row.shape[1]
    same = iota((n, width), 0) == iota((n, width), 1)
    return jnp.sum(jnp.where(same, row, jnp.zeros_like(row)), axis=1, keepdims=True)


def kernel(
    sizes,
    tok_hbm, hop_hbm, pq_hbm, qv_hbm, gain_a_hbm, gain_o_hbm,
    x_hbm, wqkv_hbm, wout_hbm, wup_hbm, wdown_hbm, slab_hbm,
    out_ref,
    tok_ref, hop_ref, pq_ref, qv_ref, gain_a_ref, gain_o_ref,
    x, wqkv, wout, wup, wdown, slab,
    qkv, ctx, hid, act, ffp, ffr, pool_y, pool_c, hop_y, hop_c, lse,
    load_sem, w1s, w1r, w2s, w2r, cs, cr, fs, fr,
    hys, hyr, hcs, hcr, pys, pyr, pcs, pcr, ls, lr, known,
):
    n_corpus, n_batch, n_tensor, texts, seq, width = sizes
    c = lax.axis_index("corpus")
    b = lax.axis_index("batch")
    t = lax.axis_index("tensor")
    core = lax.rem(c, 2)
    sibling = c + 1 - 2 * core
    heads_here = wqkv.shape[0] // (3 * HEAD_DIM)
    inner = heads_here * HEAD_DIM
    ff_here = wup.shape[1]
    passages = slab.shape[0]
    questions = qv_ref.shape[0]
    paths = n_corpus * texts
    piece = ctx.shape[-1]
    own_pass = (c * n_tensor + t) * passages

    def y_peer(d):
        return (c, b, lax.rem(t + d, n_tensor))

    def c_peer(e, d=0):
        return (lax.rem(c + e, n_corpus), b, lax.rem(t + d, n_tensor))

    def chips_away(e):
        return min(e // 2, (n_corpus - e) // 2)

    def remote(src, dst, s, r, dev):
        return pltpu.make_async_remote_copy(
            src_ref=src, dst_ref=dst, send_sem=s, recv_sem=r, device_id=dev, device_id_type=MESH
        )

    def wait_all(buf, sem):
        there = buf.at[pl.ds(1, buf.shape[0] - 1)]
        remote(there, there, sem, sem, y_peer(1)).wait_recv()

    far_first = sorted(range(1, n_corpus), key=lambda e: -chips_away(e))
    far_first_all = sorted(
        [(e, d) for e in range(n_corpus) for d in range(n_tensor) if e or d],
        key=lambda p: -chips_away(p[0]) - min(p[1], n_tensor - p[1]),
    )

    barrier = pltpu.get_barrier_semaphore()
    peers = [y_peer(d) for d in range(1, n_tensor)] + [(sibling, b, lax.rem(t + d, n_tensor)) for d in range(n_tensor)]
    peers += [c_peer(2), c_peer(n_corpus - 2)]
    for dev in peers:
        pl.semaphore_signal(barrier, inc=1, device_id=dev, device_id_type=MESH)

    def tell(stage, chips):
        for e in (2 * chips, n_corpus - 2 * chips):
            pl.semaphore_signal(known.at[stage], inc=1, device_id=c_peer(e), device_id_type=MESH)

    loads = []
    for i, (src, dst) in enumerate((
        (x_hbm, x), (wqkv_hbm, wqkv), (wout_hbm, wout.at[0]), (tok_hbm, tok_ref), (gain_a_hbm, gain_a_ref),
        (gain_o_hbm, gain_o_ref), (hop_hbm, hop_ref), (pq_hbm, pq_ref), (qv_hbm, qv_ref),
        (slab_hbm, slab), (wup_hbm, wup), (wdown_hbm, wdown),
    )):
        loads.append(pltpu.make_async_copy(src, dst, load_sem.at[i]))
    load_x, load_qkv = loads[:2]
    load_small = loads[2:9]
    load_slab, load_up, load_down = loads[9:]
    for copy in loads[:9]:
        copy.start()
    pl.semaphore_wait(barrier, len(peers))

    half = width // 2
    half_cols = pl.ds(pl.multiple_of(core * half, 128), half)
    leg1 = [
        remote(wout_hbm.at[:, half_cols], wout.at[d, :, half_cols], w1s.at[d - 1], w1r.at[d - 1], y_peer(d))
        for d in range(1, n_tensor)
    ]
    for copy in leg1:
        copy.start()
    tell(0, 1)

    load_x.wait()
    load_qkv.wait()
    for copy in (load_slab, load_up, load_down):
        copy.start()
    qkv[...] = dot(wqkv[...], x[...], 1, 1).astype(BF16)
    for copy in load_small:
        copy.wait()
    gain_a = jnp.concatenate([gain_a_ref[r:r + 1, :] for r in range(width // 128)], axis=1)
    gain_o = jnp.concatenate([gain_o_ref[r:r + 1, :] for r in range(width // 128)], axis=1)
    real = tok_ref[...] != 1
    counts = jnp.sum(real.astype(F32), axis=1, keepdims=True)

    split = seq // piece
    ctx_sends = []
    for i in range(texts):
        cols = slice(i * seq, (i + 1) * seq)
        keep = iota((seq, 1), 0).astype(F32) < counts[i:i + 1, :]
        for h in range(heads_here):
            lo = h * HEAD_DIM
            q = qkv[lo:lo + HEAD_DIM, cols] * jnp.asarray(HEAD_DIM ** -0.5, BF16)
            k = qkv[inner + lo:inner + lo + HEAD_DIM, cols]
            v = qkv[2 * inner + lo:2 * inner + lo + HEAD_DIM, cols]
            logits = dot(k, q, 0, 0)
            logits = jnp.where(keep, logits, -jnp.inf)
            weights = jnp.exp(logits - jnp.max(logits, axis=0, keepdims=True))
            weights = (weights * (1.0 / jnp.sum(weights, axis=0, keepdims=True))).astype(BF16)
            context = dot(v, weights, 1, 0).astype(BF16)
            for j in range(split):
                ctx[0, i * split + j, lo:lo + HEAD_DIM, :] = context[:, j * piece:(j + 1) * piece]
        for p in range(i * split, (i + 1) * split):
            group = [
                remote(ctx.at[0, p], ctx.at[d, p], cs.at[p, d - 1], cr.at[p, d - 1], y_peer(d))
                for d in range(1, n_tensor)
            ]
            for copy in group:
                copy.start()
            ctx_sends.append(group)

    pl.semaphore_wait(known.at[0], 2)
    tell(1, 2)

    load_slab.wait()
    pq = pq_ref[...]
    member = iota((questions, paths), 0) == pq
    before = jnp.sum((pq < iota((questions, paths), 0)).astype(F32), axis=1, keepdims=True)
    amount = jnp.sum(member.astype(F32), axis=1, keepdims=True)
    hop_col = row_to_col(hop_ref[...].astype(F32), paths)
    here = iota((paths, passages), 1).astype(F32) == hop_col - own_pass.astype(F32)
    picked = dot(here.astype(F32).astype(BF16), slab[...], 1, 0)
    question_rows = dot(member.astype(F32).astype(BF16), qv_ref[...], 0, 0)
    hop_y[0] = col_to_row(jnp.sum(picked * question_rows, axis=1, keepdims=True), 128)
    hop_sends = [
        remote(hop_y.at[0], hop_y.at[d], hys.at[d - 1], hyr, y_peer(d)) for d in range(1, n_tensor)
    ]
    for copy in hop_sends:
        copy.start()

    leg2 = []
    for d in (1, n_tensor - 1, 2):
        if d == 2:
            pl.semaphore_wait(known.at[1], 2)
            tell(2, 1)
        leg1[d - 1].wait_recv()
        copy = remote(wout.at[d, :, half_cols], wout.at[d, :, half_cols], w2s.at[d - 1], w2r.at[d - 1], (sibling, b, t))
        copy.start()
        leg2.append(copy)
    load_up.wait()
    load_down.wait()
    for copy in leg2:
        copy.wait_recv()

    rows = piece // n_tensor
    ff_sends = []
    for p in range(texts * split):
        piece_rows = slice(p * piece, (p + 1) * piece)
        attended = x[piece_rows, :].astype(F32)
        for d in range(n_tensor):
            if d:
                ctx_sends[p][d - 1].wait_recv()
            attended = attended + dot(ctx[d, p], wout[d], 0, 0)
        hid[piece_rows, :] = layer_norm(attended, gain_a).astype(BF16)
        for n in range(0, ff_here, 256):
            up = dot(hid[piece_rows, :], wup[:, n:n + 256], 1, 0)
            act[:, n:n + 256] = gelu(up).astype(BF16)
        ffp[p] = dot(act[...], wdown[...], 1, 0).astype(BF16)
        group = []
        for d in range(1, n_tensor):
            owner = lax.rem(t + d, n_tensor)
            copy = remote(
                ffp.at[p, pl.ds(pl.multiple_of(owner * rows, 16), rows)], ffr.at[p, d - 1],
                fs.at[p, d - 1], fr.at[p], y_peer(d),
            )
            copy.start()
            group.append(copy)
        ff_sends.append(group)
        if p == 0:
            pl.semaphore_wait(known.at[2], 2)
            wait_all(hop_y, hyr)
            hop_c[0] = jnp.sum(hop_y[...], axis=0)
            hopc_sends = [
                remote(hop_c.at[0], hop_c.at[e], hcs.at[e - 1], hcr, c_peer(e)) for e in far_first
            ]
            for copy in hopc_sends:
                copy.start()

    sums = [None] * texts
    for p in range(texts * split):
        i, j = p // split, p % split
        own = pl.ds(pl.multiple_of(t * rows, 16), rows)
        own_hid = pl.ds(pl.multiple_of(p * piece + t * rows, 16), rows)
        remote(ffr.at[p], ffr.at[p], fs.at[p, 0], fr.at[p], y_peer(1)).wait_recv()
        total = hid[own_hid, :].astype(F32) + ffp[p, own, :].astype(F32)
        for d in range(1, n_tensor):
            total = total + ffr[p, d - 1].astype(F32)
        encoded = layer_norm(total, gain_o)
        keep = (j * piece + t * rows + iota((rows, 1), 0)).astype(F32) < counts[i:i + 1, :]
        part = jnp.sum(jnp.where(keep, encoded, 0.0), axis=0, keepdims=True)
        sums[i] = part if sums[i] is None else sums[i] + part
    pool_y[0] = jnp.concatenate(sums, axis=0) / counts
    pool_sends = [
        remote(pool_y.at[0], pool_y.at[d], pys.at[d - 1], pyr, y_peer(d)) for d in range(1, n_tensor)
    ]
    for copy in pool_sends:
        copy.start()
    wait_all(pool_y, pyr)
    pool_c[0] = jnp.sum(pool_y[...], axis=0).astype(BF16).astype(F32)
    poolc_sends = [
        remote(pool_c.at[0], pool_c.at[e], pcs.at[e - 1], pcr, c_peer(e)) for e in far_first
    ]
    for copy in poolc_sends:
        copy.start()

    wait_all(hop_c, hcr)
    hop_row = jnp.sum(hop_c[...], axis=0)[:, :paths]
    path_at = iota((questions, paths), 1).astype(F32)
    slot = iota((questions, paths), 1)
    slot_path = lax.rem(2 * paths + texts * c - slot + 2 * lax.rem(slot, texts), paths).astype(F32)
    hops, valid, picks = [], [], []
    for k in range(HOPS):
        ok = amount > k
        hops.append(jnp.sum(jnp.where(path_at == before + k, hop_row, 0.0), axis=1, keepdims=True))
        valid.append(ok)
        picks.append(jnp.where((slot_path == before + k) & ok, 1.0, 0.0))
    pick = jnp.concatenate(picks, axis=0).astype(BF16)

    wait_all(pool_c, pcr)
    pooled = pool_c[...].reshape(paths, width)
    queries = (pooled * lax.rsqrt(jnp.sum(pooled * pooled, axis=-1, keepdims=True) + 1e-06)).astype(BF16)
    chosen = dot(pick, queries, 1, 0).astype(BF16)
    direct = dot(chosen, slab[...], 1, 1)
    scores = [
        jnp.where(valid[k], hops[k] + score_gain * direct[k * questions:(k + 1) * questions], -jnp.inf)
        for k in range(HOPS)
    ]
    top = functools.reduce(jnp.maximum, scores)
    marginal = top + jnp.log(sum(jnp.exp(s - top) for s in scores))
    local_top = jnp.max(marginal, axis=1, keepdims=True)
    local_lse = local_top + jnp.log(jnp.sum(jnp.exp(marginal - local_top), axis=1, keepdims=True))

    lse[0] = col_to_row(local_lse, 128)
    lse_sends = [
        remote(lse.at[0], lse.at[k + 1], ls.at[k], lr, c_peer(e, d)) for k, (e, d) in enumerate(far_first_all)
    ]
    for copy in lse_sends:
        copy.start()
    wait_all(lse, lr)
    parts = lse[...]
    most = jnp.max(parts, axis=0)
    norm = most + jnp.log(jnp.sum(jnp.exp(parts - most[None]), axis=0))
    out_ref[...] = marginal - row_to_col(norm, questions)

    for group in [leg1, leg2, hop_sends, hopc_sends, pool_sends, poolc_sends, lse_sends] + ctx_sends + ff_sends:
        for copy in group:
            copy.wait_send()


def shards(mesh_sizes, states, token_ids, hop_passages, path_question, question_vecs, passage_slab,
           w_qkv, w_out, w_up, w_down, gain_attn, gain_out):
    n_corpus, n_batch, n_tensor = mesh_sizes
    texts, seq, width = states.shape[1:]
    total = texts * seq
    passages = passage_slab.shape[0]
    questions = question_vecs.shape[1]
    inner = w_qkv.shape[2]
    ff_here = w_up.shape[1]
    sizes = (n_corpus, n_batch, n_tensor, texts, seq, width)
    ny, nc = n_tensor - 1, n_corpus - 1
    pieces = total // PIECE
    dma = pltpu.SemaphoreType.DMA
    vmem = pl.BlockSpec(memory_space=pltpu.VMEM)
    hbm = pl.BlockSpec(memory_space=pl.ANY)
    result = pl.pallas_call(
        functools.partial(kernel, sizes),
        out_shape=jax.ShapeDtypeStruct((questions, passages), F32),
        in_specs=[hbm] * 12,
        out_specs=vmem,
        scratch_shapes=[
            pltpu.VMEM((texts, seq), jnp.int32),
            pltpu.VMEM((1, n_corpus * texts), jnp.int32),
            pltpu.VMEM((1, n_corpus * texts), jnp.int32),
            pltpu.VMEM((questions, width), BF16),
            pltpu.VMEM((width // 128, 128), F32),
            pltpu.VMEM((width // 128, 128), F32),
            pltpu.VMEM((total, width), BF16),
            pltpu.VMEM((3 * inner, width), BF16),
            pltpu.VMEM((n_tensor, inner, width), BF16),
            pltpu.VMEM((width, ff_here), BF16),
            pltpu.VMEM((ff_here, width), BF16),
            pltpu.VMEM((passages, width), BF16),
            pltpu.VMEM((3 * inner, total), BF16),
            pltpu.VMEM((n_tensor, pieces, inner, PIECE), BF16),
            pltpu.VMEM((total, width), BF16),
            pltpu.VMEM((PIECE, ff_here), BF16),
            pltpu.VMEM((pieces, PIECE, width), BF16),
            pltpu.VMEM((pieces, ny, PIECE // n_tensor, width), BF16),
            pltpu.VMEM((n_tensor, texts, width), F32),
            pltpu.VMEM((n_corpus, texts, width), F32),
            pltpu.VMEM((n_tensor, 1, 128), F32),
            pltpu.VMEM((n_corpus, 1, 128), F32),
            pltpu.VMEM((n_tensor * n_corpus, 1, 128), F32),
            dma((12,)),
            dma((ny,)), dma((ny,)), dma((ny,)), dma((ny,)),
            dma((pieces, ny)), dma((pieces, ny)), dma((pieces, ny)), dma((pieces,)),
            dma((ny,)), dma, dma((nc,)), dma,
            dma((ny,)), dma, dma((nc,)), dma,
            dma((n_tensor * n_corpus - 1,)), dma,
            pltpu.SemaphoreType.REGULAR((3,)),
        ],
        compiler_params=pltpu.CompilerParams(
            collective_id=0, has_side_effects=True, vmem_limit_bytes=60 * 1024 * 1024
        ),
        name="hop_two",
    )(
        token_ids[0], hop_passages, path_question, question_vecs[0],
        gain_attn.reshape(-1, 128), gain_out.reshape(-1, 128),
        states.reshape(total, width), jnp.transpose(w_qkv, (1, 2, 0)).reshape(3 * inner, width),
        w_out, w_up, w_down, passage_slab,
    )
    return result[None]


def solution(mesh):
    mesh_sizes = (mesh.shape["corpus"], mesh.shape["batch"], mesh.shape["tensor"])
    return jax.shard_map(
        functools.partial(shards, mesh_sizes),
        mesh=mesh,
        in_specs=(
            P("batch", "corpus", None, None),
            P("batch", "corpus", None),
            P("batch", None),
            P("batch", None),
            P("batch", None, None),
            P(("corpus", "tensor"), None),
            P(None, None, "tensor"),
            P("tensor", None),
            P(None, "tensor"),
            P("tensor", None),
            P(),
            P(),
        ),
        out_specs=P("batch", None, ("corpus", "tensor")),
        check_vma=False,
    )
```

time: 67.3 us -> 55.4 us (0.82)
  local copies, waits for them, and re-layouts: 10.6 us -> 1.57 us
  Pallas kernels: 56.2 us -> 53.7 us
    unnamed x19 -> x1, local copies, waits for them, and re-layouts: 9.19 us -> 1.57 us
    pallas_call x1, Pallas kernels: 56.2 us -> 53.7 us  [shards(): pl.pallas_call(functools.partial(kernel, sizes), out_shape=jax.ShapeDtype...]
    broadcast_in_dim x2 -> x0, local copies, waits for them, and re-layouts: 1.38 us -> none  [the longest x1 0.69 us: shards(): gain_out[None]]
where the time goes in v2:
time: 55.4 us; the launch traced here: 55.3 us
  Pallas kernels  53.7 us (97%)
  local copies, waits for them, and re-layouts  1.57 us (3%)
    pallas_call x1, Pallas kernels, shards(): pl.pallas_call(functools.partial(kernel, sizes), out_shape=jax.ShapeDtype...  53.7 us
    unnamed x1, local copies, waits for them, and re-layouts  1.57 us

profile of v2, /device:TPU:1, one launch (start us, length us, event | category | flops | bytes accessed | tf_op | source)
XLA Modules:
  0.0 55.3 jit_solution(9786738112941562283)
XLA Ops:
  0.0 53.7 %hop_two.1 = f32[16,2048]{1,0:T(8,128)} custom-call(s32[2,256]{1,0:T(2,128)} %bitcast.15, s32[1,32]{1,0:T(1,128)} %hop_hbm.1, s32[1,32]{1,0:T(1,128)} %pq_hbm.1, bf16[16,768]{1,0:T(8,128)(2,1)} %bitcast.12, f32[6,128]{1,0:T(8,128)} %bitcast.13, f32[6,128]{1,0:T(8,128)} %bitcast.14, bf16[512,768]{1,0:T(8,128)(2,1)} %bitcast.10, bf16[576,768]{1,0:T(8,128)(2,1)} %bitcast.9, ...), custom_call_target="tpu_custom_call" | custom-call | tf_op jit(solution)/shard_map/hop_two/pallas_call | solution.py:326
  53.7 1.6 %copy.14 = f32[1,16,2048]{2,1,0:T(8,128)} copy(f32[1,16,2048]{2,1,0:T(8,128)} %bitcast.11) | data formatting | bytes 262144

commit v3 on v2

--- a/solution.py
+++ b/solution.py
@@ -56,7 +56,7 @@
     tok_ref, hop_ref, pq_ref, qv_ref, gain_a_ref, gain_o_ref,
     x, wqkv, wout, wup, wdown, slab,
     qkv, ctx, hid, act, ffp, ffr, pool_y, pool_c, hop_y, hop_c, lse,
-    load_sem, w1s, w1r, w2s, w2r, cs, cr, fs, fr,
+    load_sem, w1s, w1r, w2s, w2r, w3s, w3r, cs, cr, fs, fr,
     hys, hyr, hcs, hcr, pys, pyr, pcs, pcr, ls, lr, known,
 ):
     n_corpus, n_batch, n_tensor, texts, seq, width = sizes
@@ -80,6 +80,9 @@
     def c_peer(e, d=0):
         return (lax.rem(c + e, n_corpus), b, lax.rem(t + d, n_tensor))
 
+    def x_peer(f):
+        return (c, lax.rem(b + f, n_batch), t)
+
     def chips_away(e):
         return min(e // 2, (n_corpus - e) // 2)
 
@@ -100,7 +103,7 @@
 
     barrier = pltpu.get_barrier_semaphore()
     peers = [y_peer(d) for d in range(1, n_tensor)] + [(sibling, b, lax.rem(t + d, n_tensor)) for d in range(n_tensor)]
-    peers += [c_peer(2), c_peer(n_corpus - 2)]
+    peers += [c_peer(2), c_peer(n_corpus - 2), x_peer(1), x_peer(n_batch - 1)]
     for dev in peers:
         pl.semaphore_signal(barrier, inc=1, device_id=dev, device_id_type=MESH)
 
@@ -124,8 +127,14 @@
 
     half = width // 2
     half_cols = pl.ds(pl.multiple_of(core * half, 128), half)
+    other_cols = pl.ds(pl.multiple_of((1 - core) * half, 128), half)
+    odd = lax.rem(b, 2)
+    quarter = inner // 4
+    own_rows = pl.ds(pl.multiple_of(odd * 2 * quarter, 16), 2 * quarter)
+    own_part = [pl.ds(pl.multiple_of(odd * 2 * quarter + k * quarter, 16), quarter) for k in range(2)]
+    next_part = [pl.ds(pl.multiple_of((1 - odd) * 2 * quarter + k * quarter, 16), quarter) for k in range(2)]
     leg1 = [
-        remote(wout_hbm.at[:, half_cols], wout.at[d, :, half_cols], w1s.at[d - 1], w1r.at[d - 1], y_peer(d))
+        remote(wout_hbm.at[own_rows, half_cols], wout.at[d, own_rows, half_cols], w1s.at[d - 1], w1r.at[d - 1], y_peer(d))
         for d in range(1, n_tensor)
     ]
     for copy in leg1:
@@ -166,13 +175,17 @@
                 remote(ctx.at[0, p], ctx.at[d, p], cs.at[p, d - 1], cr.at[p, d - 1], y_peer(d))
                 for d in range(1, n_tensor)
             ]
-            for copy in group:
-                copy.start()
             ctx_sends.append(group)
+
+    def issue(p):
+        for copy in ctx_sends[p]:
+            copy.start()
 
     pl.semaphore_wait(known.at[0], 2)
     tell(1, 2)
 
+    issue(0)
+    issue(1)
     load_slab.wait()
     pq = pq_ref[...]
     member = iota((questions, paths), 0) == pq
@@ -195,13 +208,28 @@
             pl.semaphore_wait(known.at[1], 2)
             tell(2, 1)
         leg1[d - 1].wait_recv()
-        copy = remote(wout.at[d, :, half_cols], wout.at[d, :, half_cols], w2s.at[d - 1], w2r.at[d - 1], (sibling, b, t))
-        copy.start()
-        leg2.append(copy)
+        group = [
+            remote(wout.at[d, own_part[k], half_cols], wout.at[d, own_part[k], half_cols], w2s.at[d - 1, k], w2r.at[k], x_peer(f))
+            for k, f in ((0, 1), (1, n_batch - 1))
+        ]
+        group.append(remote(wout.at[d, own_rows, half_cols], wout.at[d, own_rows, half_cols], w2s.at[d - 1, 2], w3r, (sibling, b, t)))
+        for copy in group:
+            copy.start()
+        leg2 += group
+    issue(2)
+    issue(3)
     load_up.wait()
     load_down.wait()
-    for copy in leg2:
-        copy.wait_recv()
+
+    for k, f in ((0, 1), (1, n_batch - 1)):
+        there = wout.at[1:n_tensor, next_part[k], half_cols]
+        remote(there, there, w2s.at[0, k], w2r.at[k], x_peer(f)).wait_recv()
+        copy = remote(there, there, w3s.at[k], w3r, (sibling, b, t))
+        copy.start()
+        leg2.append(copy)
+    there = wout.at[1:n_tensor, :, other_cols]
+    remote(there, there, w3s.at[0], w3r, (sibling, b, t)).wait_recv()
+
 
     rows = piece // n_tensor
     ff_sends = []
@@ -303,7 +331,7 @@
     norm = most + jnp.log(jnp.sum(jnp.exp(parts - most[None]), axis=0))
     out_ref[...] = marginal - row_to_col(norm, questions)
 
-    for group in [leg1, leg2, hop_sends, hopc_sends, pool_sends, poolc_sends, lse_sends] + ctx_sends + ff_sends:
+    for group in [leg1, leg2, hop_sends, hopc_sends, pool_sends, poolc_sends, lse_sends] + ctx_sends[0:] + ff_sends:
         for copy in group:
             copy.wait_send()
 
@@ -353,7 +381,7 @@
             pltpu.VMEM((n_corpus, 1, 128), F32),
             pltpu.VMEM((n_tensor * n_corpus, 1, 128), F32),
             dma((12,)),
-            dma((ny,)), dma((ny,)), dma((ny,)), dma((ny,)),
+            dma((ny,)), dma((ny,)), dma((ny, 3)), dma((2,)), dma((2,)), dma,
             dma((pieces, ny)), dma((pieces, ny)), dma((pieces, ny)), dma((pieces,)),
             dma((ny,)), dma, dma((nc,)), dma,
             dma((ny,)), dma, dma((nc,)), dma,

time: 55.4 us -> 52 us (0.939)
  Pallas kernels: 53.7 us -> 50.3 us
    pallas_call x1, Pallas kernels: 53.7 us -> 50.3 us  [shards(): pl.pallas_call(functools.partial(kernel, sizes), out_shape=jax.ShapeDtype...]
where the time goes in v3:
time: 52 us; the launch traced here: 51.9 us
  Pallas kernels  50.3 us (97%)
  local copies, waits for them, and re-layouts  1.57 us (3%)
    pallas_call x1, Pallas kernels, shards(): pl.pallas_call(functools.partial(kernel, sizes), out_shape=jax.ShapeDtype...  50.3 us
    unnamed x1, local copies, waits for them, and re-layouts  1.57 us

profile of v3, /device:TPU:1, one launch (start us, length us, event | category | flops | bytes accessed | tf_op | source)
XLA Modules:
  0.0 51.9 jit_solution(4796919737756051424)
XLA Ops:
  0.0 50.3 %hop_two.1 = f32[16,2048]{1,0:T(8,128)} custom-call(s32[2,256]{1,0:T(2,128)} %bitcast.15, s32[1,32]{1,0:T(1,128)} %hop_hbm.1, s32[1,32]{1,0:T(1,128)} %pq_hbm.1, bf16[16,768]{1,0:T(8,128)(2,1)} %bitcast.12, f32[6,128]{1,0:T(8,128)} %bitcast.13, f32[6,128]{1,0:T(8,128)} %bitcast.14, bf16[512,768]{1,0:T(8,128)(2,1)} %bitcast.10, bf16[576,768]{1,0:T(8,128)(2,1)} %bitcast.9, ...), custom_call_target="tpu_custom_call" | custom-call | tf_op jit(solution)/shard_map/hop_two/pallas_call | solution.py:354
  50.3 1.6 %copy.14 = f32[1,16,2048]{2,1,0:T(8,128)} copy(f32[1,16,2048]{2,1,0:T(8,128)} %bitcast.11) | data formatting | bytes 262144

commit v4 on v3

--- a/solution.py
+++ b/solution.py
@@ -54,10 +54,10 @@
     x_hbm, wqkv_hbm, wout_hbm, wup_hbm, wdown_hbm, slab_hbm,
     out_ref,
     tok_ref, hop_ref, pq_ref, qv_ref, gain_a_ref, gain_o_ref,
-    x, wqkv, wout, wup, wdown, slab,
-    qkv, ctx, hid, act, ffp, ffr, pool_y, pool_c, hop_y, hop_c, lse,
-    load_sem, w1s, w1r, w2s, w2r, w3s, w3r, cs, cr, fs, fr,
-    hys, hyr, hcs, hcr, pys, pyr, pcs, pcr, ls, lr, known,
+    x, wqkv, wout, wup, wdown, slab, slab_t,
+    qkv, ctx, hid, act, ffp, ffr, opp, partial, pool, hop_y, hop_c, lse,
+    load_sem, w1s, w1r, w2s, w2r, w3s, w3r, cs, cr, fs, fr, oppr,
+    hys, hyr, hcs, hcr, ps, pr, ls, lr, known,
 ):
     n_corpus, n_batch, n_tensor, texts, seq, width = sizes
     c = lax.axis_index("corpus")
@@ -154,7 +154,6 @@
     counts = jnp.sum(real.astype(F32), axis=1, keepdims=True)
 
     split = seq // piece
-    ctx_sends = []
     for i in range(texts):
         cols = slice(i * seq, (i + 1) * seq)
         keep = iota((seq, 1), 0).astype(F32) < counts[i:i + 1, :]
@@ -170,12 +169,13 @@
             context = dot(v, weights, 1, 0).astype(BF16)
             for j in range(split):
                 ctx[0, i * split + j, lo:lo + HEAD_DIM, :] = context[:, j * piece:(j + 1) * piece]
-        for p in range(i * split, (i + 1) * split):
-            group = [
-                remote(ctx.at[0, p], ctx.at[d, p], cs.at[p, d - 1], cr.at[p, d - 1], y_peer(d))
-                for d in range(1, n_tensor)
-            ]
-            ctx_sends.append(group)
+    steps = (2, 1, 3, 0)
+    ctx_sends = {}
+    for k in steps:
+        ctx_sends[k] = []
+        for d in range(1, n_tensor):
+            q = lax.rem(t + d + k, n_tensor)
+            ctx_sends[k].append(remote(ctx.at[0, q], ctx.at[d, k], cs.at[k, d - 1], cr.at[k, d - 1], y_peer(d)))
 
     def issue(p):
         for copy in ctx_sends[p]:
@@ -184,8 +184,8 @@
     pl.semaphore_wait(known.at[0], 2)
     tell(1, 2)
 
-    issue(0)
-    issue(1)
+    for k in steps:
+        issue(k)
     load_slab.wait()
     pq = pq_ref[...]
     member = iota((questions, paths), 0) == pq
@@ -216,8 +216,8 @@
         for copy in group:
             copy.start()
         leg2 += group
-    issue(2)
-    issue(3)
+    for n in range(0, passages, 256):
+        slab_t[:, n:n + 256] = slab[n:n + 256, :].T
     load_up.wait()
     load_down.wait()
 
@@ -231,31 +231,34 @@
     remote(there, there, w3s.at[0], w3r, (sibling, b, t)).wait_recv()
 
 
-    rows = piece // n_tensor
     ff_sends = []
-    for p in range(texts * split):
-        piece_rows = slice(p * piece, (p + 1) * piece)
-        attended = x[piece_rows, :].astype(F32)
-        for d in range(n_tensor):
-            if d:
-                ctx_sends[p][d - 1].wait_recv()
-            attended = attended + dot(ctx[d, p], wout[d], 0, 0)
-        hid[piece_rows, :] = layer_norm(attended, gain_a).astype(BF16)
+    halves = (slice(0, piece // 2), slice(piece // 2, piece))
+    for k in steps:
+        q = lax.rem(t + k, n_tensor)
+        attended = x[pl.ds(pl.multiple_of(q * piece, 16), piece), :].astype(F32)
+        attended = attended + dot(ctx[0, q], wout[0], 0, 0)
+        for d in range(1, n_tensor):
+            ctx_sends[k][d - 1].wait_recv()
+            attended = attended + dot(ctx[d, k], wout[d], 0, 0)
+        hidden = layer_norm(attended, gain_a).astype(BF16)
+        hid[...] = hidden
         for n in range(0, ff_here, 256):
-            up = dot(hid[piece_rows, :], wup[:, n:n + 256], 1, 0)
+            up = dot(hid[...], wup[:, n:n + 256], 1, 0)
             act[:, n:n + 256] = gelu(up).astype(BF16)
-        ffp[p] = dot(act[...], wdown[...], 1, 0).astype(BF16)
-        group = []
-        for d in range(1, n_tensor):
-            owner = lax.rem(t + d, n_tensor)
-            copy = remote(
-                ffp.at[p, pl.ds(pl.multiple_of(owner * rows, 16), rows)], ffr.at[p, d - 1],
-                fs.at[p, d - 1], fr.at[p], y_peer(d),
-            )
-            copy.start()
-            group.append(copy)
-        ff_sends.append(group)
-        if p == 0:
+        down = dot(act[...], wdown[...], 1, 0)
+        if k == 2:
+            ffp[1] = down.astype(BF16)
+            for r, f in ((0, 1), (1, n_tensor - 1)):
+                ff_sends.append(remote(ffp.at[1, halves[r]], opp.at[r], fs.at[1, r], oppr.at[r], y_peer(f)))
+                ff_sends[-1].start()
+        elif k:
+            late = 0 if k == 1 else 1
+            ffp[k - 1, halves[1 - late], :] = down[halves[1 - late], :].astype(BF16)
+            partial[late] = down[halves[late], :]
+            part = halves[1 - late]
+            ff_sends.append(remote(ffp.at[k - 1, part], ffr.at[k - 1, part], fs.at[k - 1, 1 - late], fr.at[k - 1], y_peer(k)))
+            ff_sends[-1].start()
+        if k == steps[0]:
             pl.semaphore_wait(known.at[2], 2)
             wait_all(hop_y, hyr)
             hop_c[0] = jnp.sum(hop_y[...], axis=0)
@@ -265,59 +268,51 @@
             for copy in hopc_sends:
                 copy.start()
 
-    sums = [None] * texts
-    for p in range(texts * split):
-        i, j = p // split, p % split
-        own = pl.ds(pl.multiple_of(t * rows, 16), rows)
-        own_hid = pl.ds(pl.multiple_of(p * piece + t * rows, 16), rows)
-        remote(ffr.at[p], ffr.at[p], fs.at[p, 0], fr.at[p], y_peer(1)).wait_recv()
-        total = hid[own_hid, :].astype(F32) + ffp[p, own, :].astype(F32)
-        for d in range(1, n_tensor):
-            total = total + ffr[p, d - 1].astype(F32)
-        encoded = layer_norm(total, gain_o)
-        keep = (j * piece + t * rows + iota((rows, 1), 0)).astype(F32) < counts[i:i + 1, :]
-        part = jnp.sum(jnp.where(keep, encoded, 0.0), axis=0, keepdims=True)
-        sums[i] = part if sums[i] is None else sums[i] + part
-    pool_y[0] = jnp.concatenate(sums, axis=0) / counts
+    for late, k in ((0, 1), (1, n_tensor - 1)):
+        part = halves[late]
+        ff_sends[late].wait_recv()
+        ffp[k - 1, part, :] = (partial[late] + opp[late].astype(F32)).astype(BF16)
+        ff_sends.append(remote(ffp.at[k - 1, part], ffr.at[k - 1, part], fs.at[k - 1, late], fr.at[k - 1], y_peer(k)))
+        ff_sends[-1].start()
+    total = hid[...].astype(F32) + down
+    for k in (1, n_tensor - 1):
+        remote(ffr.at[k - 1], ffr.at[k - 1], fs.at[k - 1, 0], fr.at[k - 1], y_peer(k)).wait_recv()
+        total = total + ffr[k - 1].astype(F32)
+    encoded = layer_norm(total, gain_o)
+    own_count = sum(jnp.where(t // split == i, counts[i:i + 1, :], 0.0) for i in range(texts))
+    keep = (lax.rem(t, split) * piece + iota((piece, 1), 0)).astype(F32) < own_count
+    me = c * n_tensor + t
+    pool[pl.ds(me, 1)] = (jnp.sum(jnp.where(keep, encoded, 0.0), axis=0, keepdims=True) / own_count)[None]
     pool_sends = [
-        remote(pool_y.at[0], pool_y.at[d], pys.at[d - 1], pyr, y_peer(d)) for d in range(1, n_tensor)
+        remote(pool.at[me], pool.at[me], ps.at[k], pr, c_peer(e, d)) for k, (e, d) in enumerate(far_first_all)
     ]
     for copy in pool_sends:
-        copy.start()
-    wait_all(pool_y, pyr)
-    pool_c[0] = jnp.sum(pool_y[...], axis=0).astype(BF16).astype(F32)
-    poolc_sends = [
-        remote(pool_c.at[0], pool_c.at[e], pcs.at[e - 1], pcr, c_peer(e)) for e in far_first
-    ]
-    for copy in poolc_sends:
         copy.start()
 
     wait_all(hop_c, hcr)
     hop_row = jnp.sum(hop_c[...], axis=0)[:, :paths]
     path_at = iota((questions, paths), 1).astype(F32)
-    slot = iota((questions, paths), 1)
-    slot_path = lax.rem(2 * paths + texts * c - slot + 2 * lax.rem(slot, texts), paths).astype(F32)
-    hops, valid, picks = [], [], []
+    hops, picks = [], []
     for k in range(HOPS):
         ok = amount > k
-        hops.append(jnp.sum(jnp.where(path_at == before + k, hop_row, 0.0), axis=1, keepdims=True))
-        valid.append(ok)
-        picks.append(jnp.where((slot_path == before + k) & ok, 1.0, 0.0))
+        hop = jnp.sum(jnp.where(path_at == before + k, hop_row, 0.0), axis=1, keepdims=True)
+        hops.append(jnp.where(ok, hop, -jnp.inf))
+        picks.append(jnp.where((path_at == before + k) & ok, 1.0, 0.0))
     pick = jnp.concatenate(picks, axis=0).astype(BF16)
 
-    wait_all(pool_c, pcr)
-    pooled = pool_c[...].reshape(paths, width)
+    others = pool.at[pl.ds(0, n_corpus * n_tensor - 1)]
+    remote(others, others, ps.at[0], pr, y_peer(1)).wait_recv()
+    pooled = jnp.sum(pool[...].reshape(paths, split, 1, width), axis=1).reshape(paths, width)
+    pooled = pooled.astype(BF16).astype(F32)
     queries = (pooled * lax.rsqrt(jnp.sum(pooled * pooled, axis=-1, keepdims=True) + 1e-06)).astype(BF16)
     chosen = dot(pick, queries, 1, 0).astype(BF16)
-    direct = dot(chosen, slab[...], 1, 1)
-    scores = [
-        jnp.where(valid[k], hops[k] + score_gain * direct[k * questions:(k + 1) * questions], -jnp.inf)
-        for k in range(HOPS)
-    ]
+    direct = dot(chosen, slab_t[...], 1, 0)
+    scores = [hops[k] + score_gain * direct[k * questions:(k + 1) * questions] for k in range(HOPS)]
     top = functools.reduce(jnp.maximum, scores)
-    marginal = top + jnp.log(sum(jnp.exp(s - top) for s in scores))
-    local_top = jnp.max(marginal, axis=1, keepdims=True)
-    local_lse = local_top + jnp.log(jnp.sum(jnp.exp(marginal - local_top), axis=1, keepdims=True))
+    inner_sum = sum(jnp.exp(s - top) for s in scores)
+    local_top = jnp.max(top, axis=1, keepdims=True)
+    local_sum = jnp.sum(inner_sum * jnp.exp(top - local_top), axis=1, keepdims=True)
+    local_lse = local_top + jnp.log(local_sum)
 
     lse[0] = col_to_row(local_lse, 128)
     lse_sends = [
@@ -325,13 +320,14 @@
     ]
     for copy in lse_sends:
         copy.start()
+    marginal = top + jnp.log(inner_sum)
     wait_all(lse, lr)
     parts = lse[...]
     most = jnp.max(parts, axis=0)
     norm = most + jnp.log(jnp.sum(jnp.exp(parts - most[None]), axis=0))
     out_ref[...] = marginal - row_to_col(norm, questions)
 
-    for group in [leg1, leg2, hop_sends, hopc_sends, pool_sends, poolc_sends, lse_sends] + ctx_sends[0:] + ff_sends:
+    for group in [leg1, leg2, hop_sends, hopc_sends, pool_sends, lse_sends, ff_sends] + list(ctx_sends.values()):
         for copy in group:
             copy.wait_send()
 
@@ -369,22 +365,24 @@
             pltpu.VMEM((width, ff_here), BF16),
             pltpu.VMEM((ff_here, width), BF16),
             pltpu.VMEM((passages, width), BF16),
+            pltpu.VMEM((width, passages), BF16),
             pltpu.VMEM((3 * inner, total), BF16),
             pltpu.VMEM((n_tensor, pieces, inner, PIECE), BF16),
-            pltpu.VMEM((total, width), BF16),
+            pltpu.VMEM((PIECE, width), BF16),
             pltpu.VMEM((PIECE, ff_here), BF16),
-            pltpu.VMEM((pieces, PIECE, width), BF16),
-            pltpu.VMEM((pieces, ny, PIECE // n_tensor, width), BF16),
-            pltpu.VMEM((n_tensor, texts, width), F32),
-            pltpu.VMEM((n_corpus, texts, width), F32),
+            pltpu.VMEM((ny, PIECE, width), BF16),
+            pltpu.VMEM((ny, PIECE, width), BF16),
+            pltpu.VMEM((2, PIECE // 2, width), BF16),
+            pltpu.VMEM((2, PIECE // 2, width), F32),
+            pltpu.VMEM((n_tensor * n_corpus, 1, width), F32),
             pltpu.VMEM((n_tensor, 1, 128), F32),
             pltpu.VMEM((n_corpus, 1, 128), F32),
             pltpu.VMEM((n_tensor * n_corpus, 1, 128), F32),
             dma((12,)),
             dma((ny,)), dma((ny,)), dma((ny, 3)), dma((2,)), dma((2,)), dma,
-            dma((pieces, ny)), dma((pieces, ny)), dma((pieces, ny)), dma((pieces,)),
+            dma((pieces, ny)), dma((pieces, ny)), dma((ny, 2)), dma((ny,)), dma((2,)),
             dma((ny,)), dma, dma((nc,)), dma,
-            dma((ny,)), dma, dma((nc,)), dma,
+            dma((n_tensor * n_corpus - 1,)), dma,
             dma((n_tensor * n_corpus - 1,)), dma,
             pltpu.SemaphoreType.REGULAR((3,)),
         ],

time: 52 us -> 51.2 us (0.985)
  Pallas kernels: 50.3 us -> 49.5 us
    pallas_call x1, Pallas kernels: 50.3 us -> 49.5 us  [shards(): pl.pallas_call(functools.partial(kernel, sizes), out_shape=jax.ShapeDtype...]
where the time goes in v4:
time: 51.2 us; the launch traced here: 51.1 us
  Pallas kernels  49.5 us (97%)
  local copies, waits for them, and re-layouts  1.57 us (3%)
    pallas_call x1, Pallas kernels, shards(): pl.pallas_call(functools.partial(kernel, sizes), out_shape=jax.ShapeDtype...  49.5 us
    unnamed x1, local copies, waits for them, and re-layouts  1.57 us

profile of v4, /device:TPU:1, one launch (start us, length us, event | category | flops | bytes accessed | tf_op | source)
XLA Modules:
  0.0 51.1 jit_solution(8123939501916716230)
XLA Ops:
  0.0 49.5 %hop_two.1 = f32[16,2048]{1,0:T(8,128)} custom-call(s32[2,256]{1,0:T(2,128)} %bitcast.15, s32[1,32]{1,0:T(1,128)} %hop_hbm.1, s32[1,32]{1,0:T(1,128)} %pq_hbm.1, bf16[16,768]{1,0:T(8,128)(2,1)} %bitcast.12, f32[6,128]{1,0:T(8,128)} %bitcast.13, f32[6,128]{1,0:T(8,128)} %bitcast.14, bf16[512,768]{1,0:T(8,128)(2,1)} %bitcast.10, bf16[576,768]{1,0:T(8,128)(2,1)} %bitcast.9, ...), custom_call_target="tpu_custom_call" | custom-call | tf_op jit(solution)/shard_map/hop_two/pallas_call | solution.py:350
  49.5 1.6 %copy.14 = f32[1,16,2048]{2,1,0:T(8,128)} copy(f32[1,16,2048]{2,1,0:T(8,128)} %bitcast.11) | data formatting | bytes 262144

commit v5 on v4

--- a/solution.py
+++ b/solution.py
@@ -184,8 +184,8 @@
     pl.semaphore_wait(known.at[0], 2)
     tell(1, 2)
 
-    for k in steps:
-        issue(k)
+    issue(2)
+    issue(1)
     load_slab.wait()
     pq = pq_ref[...]
     member = iota((questions, paths), 0) == pq
@@ -216,6 +216,9 @@
         for copy in group:
             copy.start()
         leg2 += group
+        if d == 2:
+            issue(3)
+            issue(0)
     for n in range(0, passages, 256):
         slab_t[:, n:n + 256] = slab[n:n + 256, :].T
     load_up.wait()

time: 51.2 us -> 50.2 us (0.980)
  Pallas kernels: 49.5 us -> 48.5 us
    pallas_call x1, Pallas kernels: 49.5 us -> 48.5 us  [shards(): pl.pallas_call(functools.partial(kernel, sizes), out_shape=jax.ShapeDtype...]
where the time goes in v5:
time: 50.2 us; the launch traced here: 50.1 us
  Pallas kernels  48.5 us (97%)
  local copies, waits for them, and re-layouts  1.57 us (3%)
    pallas_call x1, Pallas kernels, shards(): pl.pallas_call(functools.partial(kernel, sizes), out_shape=jax.ShapeDtype...  48.5 us
    unnamed x1, local copies, waits for them, and re-layouts  1.57 us

profile of v5, /device:TPU:1, one launch (start us, length us, event | category | flops | bytes accessed | tf_op | source)
XLA Modules:
  0.0 50.1 jit_solution(13037058780956892335)
XLA Ops:
  0.0 48.5 %hop_two.1 = f32[16,2048]{1,0:T(8,128)} custom-call(s32[2,256]{1,0:T(2,128)} %bitcast.15, s32[1,32]{1,0:T(1,128)} %hop_hbm.1, s32[1,32]{1,0:T(1,128)} %pq_hbm.1, bf16[16,768]{1,0:T(8,128)(2,1)} %bitcast.12, f32[6,128]{1,0:T(8,128)} %bitcast.13, f32[6,128]{1,0:T(8,128)} %bitcast.14, bf16[512,768]{1,0:T(8,128)(2,1)} %bitcast.10, bf16[576,768]{1,0:T(8,128)(2,1)} %bitcast.9, ...), custom_call_target="tpu_custom_call" | custom-call | tf_op jit(solution)/shard_map/hop_two/pallas_call | solution.py:353
  48.5 1.6 %copy.14 = f32[1,16,2048]{2,1,0:T(8,128)} copy(f32[1,16,2048]{2,1,0:T(8,128)} %bitcast.11) | data formatting | bytes 262144

commit v6 on v5

--- a/solution.py
+++ b/solution.py
@@ -261,7 +261,7 @@
             part = halves[1 - late]
             ff_sends.append(remote(ffp.at[k - 1, part], ffr.at[k - 1, part], fs.at[k - 1, 1 - late], fr.at[k - 1], y_peer(k)))
             ff_sends[-1].start()
-        if k == steps[0]:
+        if k == steps[-1]:
             pl.semaphore_wait(known.at[2], 2)
             wait_all(hop_y, hyr)
             hop_c[0] = jnp.sum(hop_y[...], axis=0)

time: 50.2 us -> 50.2 us (level)
  no operation moved by 1% of the time
where the time goes in v6:
time: 50.2 us; the launch traced here: 50.1 us
  Pallas kernels  48.5 us (97%)
  local copies, waits for them, and re-layouts  1.57 us (3%)
    pallas_call x1, Pallas kernels, shards(): pl.pallas_call(functools.partial(kernel, sizes), out_shape=jax.ShapeDtype...  48.5 us
    unnamed x1, local copies, waits for them, and re-layouts  1.57 us

profile of v6, /device:TPU:1, one launch (start us, length us, event | category | flops | bytes accessed | tf_op | source)
XLA Modules:
  0.0 50.1 jit_solution(7429855497201376507)
XLA Ops:
  0.0 48.5 %hop_two.1 = f32[16,2048]{1,0:T(8,128)} custom-call(s32[2,256]{1,0:T(2,128)} %bitcast.15, s32[1,32]{1,0:T(1,128)} %hop_hbm.1, s32[1,32]{1,0:T(1,128)} %pq_hbm.1, bf16[16,768]{1,0:T(8,128)(2,1)} %bitcast.12, f32[6,128]{1,0:T(8,128)} %bitcast.13, f32[6,128]{1,0:T(8,128)} %bitcast.14, bf16[512,768]{1,0:T(8,128)(2,1)} %bitcast.10, bf16[576,768]{1,0:T(8,128)(2,1)} %bitcast.9, ...), custom_call_target="tpu_custom_call" | custom-call | tf_op jit(solution)/shard_map/hop_two/pallas_call | solution.py:353
  48.5 1.6 %copy.14 = f32[1,16,2048]{2,1,0:T(8,128)} copy(f32[1,16,2048]{2,1,0:T(8,128)} %bitcast.11) | data formatting | bytes 262144
